TPU v7x, 32 devices: a whole 2x2x4 slice. The times are simulated.
32 devices in a mesh: row: 4 (over y, x), blk: 8 (over z, core).
Axes of the slice: x: 2, y: 2, z: 4, core: 2. Of those that a mesh axis runs over, the one named last changes fastest.
Arguments:
- spike_counts: int32 [16384, 2048], P(('row', 'blk')), may hold values from 0 to 23, as said below
- kernel_taps: int32 [16], replicated, may hold values from 1 to 8
- lag_bins: int32 [2], replicated, may hold values from 1 to 32, as said below
Outputs:
- correlogram: bfloat16 [2, 16384, 4, 4096], P(None, 'row', None, 'blk')
Inputs may be any that keep to these rules, and one draw needn't show every extreme that they name: `spike_counts`: neurons fire at different rates and share a common drive. `lag_bins`: the second lag equals 32; the first lies between 1 and 31.
All inputs are finite; a program needn't handle non-finite values.
Results may differ from a plain program's by a relative error of at most 0.0034.
Values may be sent and summed in bfloat16 or wider, within the bound.
No kernel may reach another device: no remote copies, remote signals or barrier semaphores. Data moves between devices by JAX's collectives and lax.ppermute only.
A program may use at most 192 MiB of HBM per device.

v0:
```python
import jax
import jax.numpy as jnp
from jax import lax
from jax.sharding import PartitionSpec as P

NEURONS = 16384
BINS = 2048
TAPS = 16


def smoothed(spike_counts, kernel_taps):
    counts = spike_counts.astype(jnp.float32)
    weights = kernel_taps.astype(jnp.float32) / jnp.sum(kernel_taps.astype(jnp.float32))
    padded = jnp.pad(counts, ((0, 0), (TAPS - 1, 0)))
    result = jnp.zeros_like(counts)
    for delay in range(TAPS):
        result = result + weights[delay] * padded[:, TAPS - 1 - delay : TAPS - 1 - delay + BINS]
    return result


def later_bins(data, lag):
    padded = jnp.pad(data, ((0, 0), (0, BINS)))
    return lax.dynamic_slice_in_dim(padded, lag, BINS, 1)


def shards(spike_counts, kernel_taps, lag_bins):
    smooth = smoothed(spike_counts, kernel_taps)
    centred = smooth - jnp.mean(smooth, axis=1, keepdims=True)
    totals = lax.psum(jnp.sum(centred, axis=0), ("row", "blk"))
    residual_part = centred - (totals / NEURONS)[None, :]
    zscored = (
        residual_part
        * lax.rsqrt(jnp.mean(residual_part * residual_part, axis=1, keepdims=True) + 1e-05)
    ).astype(jnp.bfloat16)
    span_rows = zscored.shape[0]
    groups = lax.axis_size("row")
    columns = lax.all_gather(zscored, "row", axis=0, tiled=True)
    stacked = jnp.concatenate(
        [later_bins(columns, lag_bins[0]), later_bins(columns, lag_bins[1])], axis=0
    )
    piece = lax.all_gather(zscored, "blk", axis=0, tiled=True)
    product = jnp.dot(piece, stacked.T, preferred_element_type=jnp.float32) / BINS
    product = product.reshape(piece.shape[0], 2, groups, span_rows)
    return jnp.transpose(product, (1, 0, 2, 3)).astype(jnp.bfloat16)


def solution(mesh):
    placed = (P(("row", "blk"), None), P(), P())
    return jax.shard_map(
        shards, mesh=mesh, in_specs=placed, out_specs=P(None, "row", None, "blk"), check_vma=False
    )
```

profile of v0, /device:TPU:17, one launch (start us, length us, event | category | flops | bytes accessed | tf_op | source)
XLA Modules:
  0.0 467.4 jit_solution(15914184754820221334)
XLA Ops:
  6.5 0.0 all-gather.5.cloned.1.call-start
  6.5 1.3 convert_reduce_fusion
  7.8 1.3 convert_divide_fusion
  9.1 0.7 fusion.8
  9.8 2.5 convert_element_type.25
  12.3 26.7 %fusion.6 = (f32[512]{0:T(512)S(1)}, f32[512,2048]{1,0:T(8,128)S(1)}) fusion(f32[]{:T(128)} %bitcast.15, f32[]{:T(128)} %bitcast.14, f32[]{:T(128)} %bitcast.13, f32[]{:T(128)} %bitcast.12, f32[]{:T(128)} %bitcast.11, f32[]{:T(128)} %bitcast.10, f32[]{:T(128)} %bitcast.9, f32[]{:T(128)} %bitcast.8, f32[]{:T(128)} %bitcast.7, f32[]{:T(128)} %bitcast.6, ...), kind=kLoop, calls=%fused_computation.19 | loop fusion | flops 33553920 | bytes 8390720 | tf_op jit(solution)/shard_map/reduce_sum | solution.py:28
  39.1 0.0 copy-start
  39.1 2.0 copy-done
  41.1 0.3 subtract_reduce_fusion
  41.4 39.6 %psum.7 = f32[2048]{0:T(1024)S(1)} all-reduce(f32[2048]{0:T(1024)S(1)} %subtract_reduce_fusion), channel_id=1, replica_groups=mesh['row'=4,'blk'=8] {'row','blk'}, use_global_device_ids=true, to_apply=%region_3.4 | all-reduce | flops 2048 | bytes 16384 | tf_op jit(solution)/shard_map/psum | solution.py:29
  81.0 0.0 copy-start.1
  81.0 3.0 multiply_reduce_fusion
  84.1 0.4 copy-done.1
  84.5 0.0 copy-start.2
  84.5 2.0 multiply_convert_fusion.1
  86.4 0.0 all-gather.5.cloned.1.call-update
  86.5 0.2 all-gather.3.cloned.1.call-start
  86.7 0.5 all-gather.3.cloned.1.call-update
  87.2 0.0 copy-done.2
  87.2 0.6 fusion.7
  91.8 83.1 %all-gather.5.cloned.1.call-done = bf16[2048,2048]{1,0:T(8,128)(2,1)} async-done(((bf16[512,2048]{1,0:T(8,128)(2,1)}), bf16[2048,2048]{1,0:T(8,128)(2,1)}) %all-gather.5.cloned.1.call-update) | async-done | bytes 8388624 | tf_op jit(solution)/shard_map/all_gather | solution.py:37
  174.9 17.3 %pad_dynamic-slice_fusion.1 = (bf16[2048,2048]{1,0:T(8,128)(2,1)}, bf16[2048,2048]{1,0:T(8,128)(2,1)}) fusion(s32[]{:T(128)S(6)} %select_n.6, bf16[2048,2048]{1,0:T(8,128)(2,1)} %all-gather.5.cloned.1.call-done, s32[]{:T(128)S(6)} %select_n.7), kind=kLoop, calls=%fused_computation.2 | loop fusion | bytes 25165832 | tf_op jit(solution)/shard_map/dynamic_slice | solution.py:23
  192.2 134.1 %all-gather.3.cloned.1.call-done = bf16[4096,2048]{1,0:T(8,128)(2,1)} async-done(((bf16[512,2048]{1,0:T(8,128)(2,1)}), bf16[4096,2048]{1,0:T(8,128)(2,1)}) %all-gather.3.cloned.1.call-update) | async-done | bytes 16777232 | tf_op jit(solution)/shard_map/all_gather | solution.py:41
  326.4 79.6 %multiply_convert_fusion = bf16[4096,4096]{0,1:T(8,128)(2,1)} fusion(bf16[4096,2048]{1,0:T(8,128)(2,1)} %all-gather.3.cloned.1.call-done, bf16[2048,2048]{1,0:T(8,128)(2,1)} %get-tuple-element.8, bf16[2048,2048]{1,0:T(8,128)(2,1)} %get-tuple-element.7), kind=kOutput, calls=%fused_computation | convolution fusion | flops 68786585600 | bytes 67108864 | tf_op jit(solution)/shard_map/dot_general | solution.py:42
  406.0 54.6 %copy.4 = bf16[4096,2,4,512]{3,2,0,1:T(4,128)(2,1)} copy(bf16[4096,2,4,512]{0,3,2,1:T(8,128)(2,1)} %bitcast.22) | data formatting | bytes 67108864 | tf_op jit(solution)/shard_map/convert_element_type | solution.py:44
  (3 shorter events, 0.0 us)
Async XLA Ops:
  6.5 168.4 %all-gather.5.cloned.1.call-start = ((), (), s32[]{:S(2)}) async-start(), calls=%async_computation.1 | async-start | bytes 10485760 | tf_op jit(solution)/shard_map/all_gather | solution.py:37
  39.1 2.0 copy-start
  81.0 3.5 copy-start.1
  84.5 2.8 copy-start.2
  86.5 239.9 %all-gather.3.cloned.1.call-start = ((), (), s32[]{:S(2)}) async-start(), calls=%async_computation | async-start | bytes 18874368 | tf_op jit(solution)/shard_map/all_gather | solution.py:41
Sparse Core Ops, SparseCore 0:
  86.6 88.3 all-gather.4
  176.5 149.7 all-gather.2
where the time goes:
time: 472 us; the launch traced here: 467 us
  waiting for transfers between devices  218 us (46%)
  matrix products  79.6 us (17%)
  local copies, waits for them, and re-layouts  75.6 us (16%)
  blocking collectives  39.6 us (8%)
  other arithmetic  37.2 us (8%)
  between operations  17.4 us (4%)
    all_gather x1, waiting for transfers between devices, shards(): piece = lax.all_gather(zscored, 'blk', axis=0, tiled=True)  134 us
    all_gather x1, waiting for transfers between devices, shards(): columns = lax.all_gather(zscored, 'row', axis=0, tiled=True)  83.1 us
    dot_general x1, matrix products, shards(): jnp.dot(piece, stacked.T, preferred_element_type=jnp.float32) / BINS  79.6 us
    convert_element_type x1, local copies, waits for them, and re-layouts, shards(): return jnp.transpose(product, (1, 0, 2, 3)).astype(jnp.bfloat16)  54.6 us
    psum x1, blocking collectives, shards(): totals = lax.psum(jnp.sum(centred, axis=0), ('row', 'blk'))  39.6 us
    reduce_sum x1, other arithmetic, shards(): centred = smooth - jnp.mean(smooth, axis=1, keepdims=True)  26.7 us
    dynamic_slice x1, local copies, waits for them, and re-layouts, later_bins(): return lax.dynamic_slice_in_dim(padded, lag, BINS, 1)  17.3 us
  transfers between devices with their start and end apart: 2, of which 2 were waited for; matrix products, arithmetic and copies ran while one was open for 4% of the time, Pallas kernels for 0%

commit v1 on v0

--- a/solution.py
+++ b/solution.py
@@ -1,11 +1,21 @@
+import functools
+
 import jax
 import jax.numpy as jnp
 from jax import lax
+from jax.experimental import pallas as pl
+from jax.experimental.pallas import tpu as pltpu
 from jax.sharding import PartitionSpec as P
 
 NEURONS = 16384
 BINS = 2048
 TAPS = 16
+AXES = ("row", "blk")
+LANES = 128
+BAND = 256
+STEP = 64
+MIB = 1 << 20
+SCALE = 1.0
 
 
 def smoothed(spike_counts, kernel_taps):
@@ -23,10 +33,10 @@
     return lax.dynamic_slice_in_dim(padded, lag, BINS, 1)
 
 
-def shards(spike_counts, kernel_taps, lag_bins):
+def gathered_shards(spike_counts, kernel_taps, lag_bins):
     smooth = smoothed(spike_counts, kernel_taps)
     centred = smooth - jnp.mean(smooth, axis=1, keepdims=True)
-    totals = lax.psum(jnp.sum(centred, axis=0), ("row", "blk"))
+    totals = lax.psum(jnp.sum(centred, axis=0), AXES)
     residual_part = centred - (totals / NEURONS)[None, :]
     zscored = (
         residual_part
@@ -44,8 +54,356 @@
     return jnp.transpose(product, (1, 0, 2, 3)).astype(jnp.bfloat16)
 
 
+def smooth_kernel(taps_ref, counts_ref, *out_refs):
+    centred_refs, total_ref = out_refs[:2], out_refs[2]
+    rows, bins = counts_ref.shape
+    at = lax.broadcasted_iota(jnp.int32, (BAND, BAND), 1) - lax.broadcasted_iota(
+        jnp.int32, (BAND, BAND), 0
+    )
+    same = jnp.zeros((BAND, BAND), jnp.float32)
+    before = jnp.zeros((BAND, BAND), jnp.float32)
+    weight = jnp.float32(0)
+    for delay in range(TAPS):
+        tap = taps_ref[delay].astype(jnp.float32)
+        weight = weight + tap
+        same = jnp.where(at == delay, tap, same)
+        before = jnp.where(at == delay - BAND, tap, before)
+    same = same.astype(jnp.bfloat16)
+    before = before.astype(jnp.bfloat16)
+    sums = []
+    last = None
+    for block in range(bins // BAND):
+        part = counts_ref[:, block * BAND : (block + 1) * BAND].astype(jnp.float32)
+        part = part.astype(jnp.bfloat16)
+        filtered = jnp.dot(part, same, preferred_element_type=jnp.float32)
+        if last is not None:
+            filtered = filtered + jnp.dot(last, before, preferred_element_type=jnp.float32)
+        sums.append(filtered)
+        last = part
+    mean = functools.reduce(
+        jnp.add, [jnp.sum(filtered, axis=1, keepdims=True) for filtered in sums]
+    ) * (1.0 / bins)
+    for block, filtered in enumerate(sums):
+        centred = (filtered - mean) / weight
+        span = slice(block * BAND, (block + 1) * BAND)
+        for number, centred_ref in enumerate(centred_refs):
+            half = centred_ref.shape[0]
+            centred_ref[:, span] = centred[number * half : (number + 1) * half].astype(
+                jnp.bfloat16
+            )
+        total_ref[:, span] = jnp.sum(centred, axis=0, keepdims=True)
+
+
+def smooth_rows(counts, taps):
+    rows, bins = counts.shape
+    half = jax.ShapeDtypeStruct((rows // 2, bins), jnp.bfloat16)
+    return pl.pallas_call(
+        smooth_kernel,
+        in_specs=[
+            pl.BlockSpec(memory_space=pltpu.SMEM),
+            pl.BlockSpec(memory_space=pltpu.VMEM),
+        ],
+        out_specs=[pl.BlockSpec(memory_space=pltpu.VMEM)] * 3,
+        out_shape=[half, half, jax.ShapeDtypeStruct((1, bins), jnp.float32)],
+        compiler_params=pltpu.CompilerParams(vmem_limit_bytes=24 * MIB),
+        cost_estimate=pl.CostEstimate(
+            flops=int(SCALE * 4 * rows * bins * BAND), bytes_accessed=int(SCALE * 6 * rows * bins), transcendentals=0
+        ),
+        name="smooth_rows",
+    )(taps, counts)
+
+
+def standardized(centred, population):
+    residual = centred.astype(jnp.float32) - population
+    power = jnp.mean(residual * residual, axis=1, keepdims=True)
+    return residual * lax.rsqrt(power + 1e-05)
+
+
+def columns_kernel(counts, place_ref, lag_ref, population_ref, *refs):
+    out_ref = refs[-1]
+    population = population_ref[...]
+    bins = population.shape[1]
+    lane = lax.broadcasted_iota(jnp.int32, (STEP, LANES), 1)
+    first = 0
+    for turn, count in enumerate(counts):
+        pieces = refs[first : first + count]
+        first += count
+
+        @pl.when(pl.program_id(0) == turn)
+        def _():
+            at = 0
+            for piece in pieces:
+                for start in range(0, piece.shape[0], STEP):
+                    score = standardized(piece[start : start + STEP, :], population)
+                    score = score.astype(jnp.bfloat16).astype(jnp.float32) * (1.0 / bins)
+                    rows = slice(at % LANES, at % LANES + STEP)
+                    for which in range(2):
+                        lag = lag_ref[which]
+                        after = jnp.zeros((STEP, LANES), jnp.float32)
+                        for tile in reversed(range(bins // LANES)):
+                            span = slice(tile * LANES, (tile + 1) * LANES)
+                            moved = pltpu.roll(score[:, span], LANES - lag, 1)
+                            merged = jnp.where(lane < LANES - lag, moved, after)
+                            out_ref[which, at // LANES, 0, rows, span] = merged.astype(
+                                jnp.bfloat16
+                            )
+                            after = moved
+                    at += STEP
+
+
+def column_groups(place, lag_bins, population, pieces, held, groups):
+    bins = population.shape[1]
+    tiles = sum(piece.shape[0] for piece in pieces[0]) // LANES
+    flat = [piece for group in pieces for piece in group]
+    whole = lambda i, place: (0, 0)
+    in_specs = [pl.BlockSpec(memory_space=pltpu.SMEM), pl.BlockSpec((1, bins), whole)]
+    in_specs += [pl.BlockSpec(piece.shape, whole) for piece in flat]
+    operands = [lag_bins, population, *flat]
+    aliases = {}
+    if held is not None:
+        in_specs.append(pl.BlockSpec(memory_space=pl.ANY))
+        operands.append(held)
+        aliases = {len(operands): 0}
+    size = len(pieces) * tiles * LANES * bins
+    return pl.pallas_call(
+        functools.partial(columns_kernel, [len(group) for group in pieces]),
+        grid_spec=pltpu.PrefetchScalarGridSpec(
+            num_scalar_prefetch=1,
+            grid=(len(pieces),),
+            in_specs=in_specs,
+            out_specs=pl.BlockSpec(
+                (2, tiles, 1, LANES, bins), lambda i, place: (0, 0, place[i], 0, 0)
+            ),
+        ),
+        out_shape=jax.ShapeDtypeStruct((2, tiles, groups, LANES, bins), jnp.bfloat16),
+        input_output_aliases=aliases,
+        compiler_params=pltpu.CompilerParams(vmem_limit_bytes=24 * MIB),
+        cost_estimate=pl.CostEstimate(
+            flops=int(SCALE * 12 * size), bytes_accessed=int(SCALE * 6 * size), transcendentals=0
+        ),
+        name="column_groups",
+    )(place, *operands)
+
+
+def product_kernel(count, wide, place_ref, spot_ref, population_ref, *refs):
+    pieces = refs[:count]
+    columns = refs[count : count + wide]
+    out_ref, scores, mixed = refs[-3:]
+    half, groups, lanes = out_ref.shape[-3:]
+    halves = out_ref.shape[3]
+    lag, tile = pl.program_id(0), pl.program_id(1)
+    tiles = columns[0].shape[1]
+
+    def standardize(number):
+        population = population_ref[...]
+        for start in range(0, half, STEP):
+            at = pl.multiple_of(spot_ref[number] + start, STEP)
+            scores[pl.ds(at, STEP), :] = standardized(
+                pieces[number][start : start + STEP, :], population
+            ).astype(jnp.bfloat16)
+
+    def multiply(right, number):
+        at = pl.multiple_of(spot_ref[number], half)
+        product = lax.dot_general(
+            scores[pl.ds(at, half), :],
+            right,
+            (((1,), (1,)), ((), ())),
+            preferred_element_type=jnp.float32,
+        )
+        base = number * half * groups
+        for group in range(groups):
+            mixed[pl.ds(base + group, half, stride=groups), :] = product[
+                :, group * lanes : (group + 1) * lanes
+            ]
+        done = mixed[base : base + half * groups, :].astype(jnp.bfloat16)
+        block = spot_ref[number] // half
+        out_ref[0, 0, block // halves, block % halves] = done.reshape(half, groups, lanes)
+
+    def all_pieces(columns_ref, fresh):
+        right = columns_ref[lag, tile % tiles].reshape(groups * lanes, columns_ref.shape[-1])
+        if fresh:
+            standardize(0)
+        for number in range(count):
+            if fresh and number + 1 < count:
+                standardize(number + 1)
+            multiply(right, number)
+
+    fresh = (lag == 0) & (tile == 0)
+    pl.when(fresh)(functools.partial(all_pieces, columns[0], True))
+    for number in range(wide):
+        mine = jnp.logical_not(fresh) & (tile // tiles == number)
+        pl.when(mine)(functools.partial(all_pieces, columns[number], False))
+
+
+def product_rows(place, spot, population, pieces, columns, which, held, shape):
+    half, bins = pieces[0].shape
+    halves = len(pieces) // 2
+    wide = len(columns)
+    _, tiles, groups, lanes, _ = columns[0].shape
+    rows = half * len(pieces)
+    operands = [population, *pieces, *columns]
+    in_specs = [pl.BlockSpec(memory_space=pltpu.VMEM) for _ in operands]
+    aliases = {}
+    if held is not None:
+        in_specs.append(pl.BlockSpec(memory_space=pl.ANY))
+        operands.append(held)
+        aliases = {2 + len(operands) - 1: 0}
+    return pl.pallas_call(
+        functools.partial(product_kernel, len(pieces), wide),
+        grid_spec=pltpu.PrefetchScalarGridSpec(
+            num_scalar_prefetch=2,
+            grid=(2, wide * tiles),
+            in_specs=in_specs,
+            out_specs=pl.BlockSpec(
+                (1, 1, 2, halves, half, groups, lanes),
+                lambda l, k, place, spot: (l, place[0], 0, place[1], 0, 0, which * tiles + k),
+            ),
+            scratch_shapes=[
+                pltpu.VMEM((rows, bins), jnp.bfloat16),
+                pltpu.VMEM((rows * groups, lanes), jnp.float32),
+            ],
+        ),
+        out_shape=jax.ShapeDtypeStruct(shape, jnp.bfloat16),
+        input_output_aliases=aliases,
+        compiler_params=pltpu.CompilerParams(vmem_limit_bytes=16 * MIB),
+        cost_estimate=pl.CostEstimate(
+            flops=int(SCALE * 4 * rows * wide * tiles * groups * lanes * bins),
+            bytes_accessed=int(SCALE * 16 * MIB),
+            transcendentals=0,
+        ),
+        name="product_rows",
+    )(place, spot, *operands)
+
+
+def pairs(target):
+    found = []
+    for row in range(4):
+        for z in range(4):
+            for core in range(2):
+                to = target(row, z, core)
+                if to is not None:
+                    found.append((row * 8 + z * 2 + core, to[0] * 8 + to[1] * 2 + to[2]))
+    return found
+
+
+ACROSS_X = pairs(lambda row, z, core: (row ^ 1, z, core))
+ACROSS_Y = pairs(lambda row, z, core: (row ^ 2, z, core))
+ACROSS_BOTH = pairs(lambda row, z, core: (row ^ 3, z, core))
+ALONG = [pairs(lambda row, z, core, n=n: (row, (z + n) % 4, core)) for n in (1, 2, 3)]
+SIBLING = pairs(lambda row, z, core: (row, z, 1 - core))
+OUTER = pairs(lambda row, z, core: (row, z ^ 1, core))
+INNER = pairs(lambda row, z, core: (row, 3 - z, core) if z in (1, 2) else None)
+OUTWARD = pairs(lambda row, z, core: (row, 0 if z == 1 else 3, core) if z in (1, 2) else None)
+
+
+def send(data, route, name):
+    with jax.named_scope(name):
+        return lax.ppermute(data, AXES, route)
+
+
+def line_shards(spike_counts, kernel_taps, lag_bins):
+    rows, bins = spike_counts.shape
+    half = rows // 2
+    groups = lax.axis_size("row")
+    row = lax.axis_index("row")
+    z = lax.axis_index("blk") // 2
+    core = lax.axis_index("blk") % 2
+    inside = (z == 1) | (z == 2)
+    low = z < 2
+
+    *own, totals = smooth_rows(spike_counts, kernel_taps)
+
+    parts = [send(totals, route, "sum_rows") for route in (ACROSS_X, ACROSS_Y, ACROSS_BOTH)]
+    summed = totals + parts[0] + parts[1] + parts[2]
+    summed = summed + send(summed, SIBLING, "sum_cores")
+    parts = [send(summed, route, "sum_line") for route in ALONG]
+    population = (summed + parts[0] + parts[1] + parts[2]) * (1.0 / NEURONS)
+
+    near, far, sib, side, flank, corner = [], [], [], [], [], []
+    for h in range(2):
+        piece = own[h]
+        if h == 1:
+            piece, _ = lax.optimization_barrier((piece, summed))
+        near.append(send(piece, OUTER, f"near_{h}"))
+        far.append(send(piece, INNER, f"far_{h}"))
+        sib.append(send(piece, SIBLING, f"sib_{h}"))
+    for h in range(2):
+        piece = own[h]
+        if h == 1:
+            piece, _ = lax.optimization_barrier((piece, corner[0]))
+        side.append(send(piece, ACROSS_X, f"side_{h}"))
+        flank.append(send(piece, ACROSS_Y, f"flank_{h}"))
+        corner.append((side[h][: half // 2], flank[h][half // 2 :]))
+    corner = [
+        (send(a, ACROSS_Y, f"corner_{h}"), send(b, ACROSS_X, f"corner_{h}"))
+        for h, (a, b) in enumerate(corner)
+    ]
+
+    far_near = [send(near[h], INNER, f"far_near_{h}") for h in range(2)]
+    out_far = [send(far[h], OUTWARD, f"out_far_{h}") for h in range(2)]
+    out_far_near = [send(far_near[h], OUTWARD, f"out_far_near_{h}") for h in range(2)]
+    second = [jnp.where(inside, far[h], out_far[h]) for h in range(2)]
+    third = [jnp.where(inside, far_near[h], out_far_near[h]) for h in range(2)]
+    near_sib = [send(near[h], SIBLING, f"near_sib_{h}") for h in range(2)]
+    second_sib = [send(second[h], SIBLING, f"second_sib_{h}") for h in range(2)]
+    third_sib = [send(third[h], SIBLING, f"third_sib_{h}") for h in range(2)]
+
+    place = jnp.stack([row, row ^ 1, row ^ 2, row ^ 3]).astype(jnp.int32)
+    columns = []
+    for h in range(2):
+        part = column_groups(
+            place[:3], lag_bins, population, [[own[h]], [side[h]], [flank[h]]], None, groups
+        )
+        part = column_groups(
+            place[3:], lag_bins, population, [list(corner[h])], part, groups
+        )
+        columns.append(part)
+
+    shape = (2, 4, 2, 2, half, groups, rows)
+    mine, other = core * rows, (1 - core) * rows
+    spot = jnp.stack([mine, mine + half, other, other + half]).astype(jnp.int32)
+    spot_half = jnp.stack([core * half, (1 - core) * half]).astype(jnp.int32)
+
+    def at(z, h):
+        return jnp.stack([z, jnp.int32(h)]).astype(jnp.int32)
+
+    out = None
+    for h in range(2):
+        for position, pieces in ((z, own + sib), (z ^ 1, near + near_sib)):
+            out = product_rows(
+                at(position, 0), spot, population, pieces, [columns[h]], h, out, shape
+            )
+    out = product_rows(
+        at(jnp.where(low, 2, 1), 0),
+        spot,
+        population,
+        second + second_sib,
+        columns,
+        0,
+        out,
+        shape,
+    )
+    for h in range(2):
+        out = product_rows(
+            at(jnp.where(low, 3, 0), h),
+            spot_half,
+            population,
+            [third[h], third_sib[h]],
+            columns,
+            0,
+            out,
+            shape,
+        )
+    return out.reshape(2, 8 * rows, groups, rows)
+
+
 def solution(mesh):
     placed = (P(("row", "blk"), None), P(), P())
+    line = mesh.shape["row"] == 4 and mesh.shape["blk"] == 8
     return jax.shard_map(
-        shards, mesh=mesh, in_specs=placed, out_specs=P(None, "row", None, "blk"), check_vma=False
+        line_shards if line else gathered_shards,
+        mesh=mesh,
+        in_specs=placed,
+        out_specs=P(None, "row", None, "blk"),
+        check_vma=False,
     )

time: 472 us -> 236 us (0.50)
  waiting for transfers between devices: 218 us -> 40.4 us
  Pallas kernels: 0 us -> 134 us
  matrix products: 79.6 us -> 0 us
  local copies, waits for them, and re-layouts: 75.6 us -> 5.72 us
  starting transfers between devices: 0.22 us -> 47.8 us
  blocking collectives: 39.6 us -> 0 us
  other arithmetic: 37.2 us -> 3.49 us
  between operations: 17.4 us -> 0.55 us
    all_gather x2 -> x0, waiting for transfers between devices: 217 us -> none  [the longest x1 134 us: shards(): piece = lax.all_gather(zscored, 'blk', axis=0, tiled=True)]
    pallas_call x0 -> x12, Pallas kernels: none -> 134 us  [the longest x7 115 us: product_rows(): pl.pallas_call(functools.partial(product_kernel, len(pieces), wide), grid...]
    dot_general x1 -> x0, matrix products: 79.6 us -> none  [shards(): jnp.dot(piece, stacked.T, preferred_element_type=jnp.float32) / BINS]
    convert_element_type x1 -> x0, local copies, waits for them, and re-layouts: 54.6 us -> none  [shards(): return jnp.transpose(product, (1, 0, 2, 3)).astype(jnp.bfloat16)]
    ppermute x0 -> x33, starting transfers between devices: none -> 47.8 us  [send(): return lax.ppermute(data, AXES, route)]
    ppermute x0 -> x33, waiting for transfers between devices: none -> 40.4 us  [send(): return lax.ppermute(data, AXES, route)]
    psum x1 -> x0, blocking collectives: 39.6 us -> none  [shards(): totals = lax.psum(jnp.sum(centred, axis=0), ('row', 'blk'))]
    reduce_sum x4 -> x0, other arithmetic: 31.4 us -> none  [the longest x1 26.7 us: shards(): centred = smooth - jnp.mean(smooth, axis=1, keepdims=True)]
  transfers between devices with their start and end apart: 2 -> 33, of which waited for: 2 -> 10; matrix products, arithmetic and copies ran while one was open for 4% -> 2% of each run, Pallas kernels for 0% -> 51%
where the time goes in v1:
time: 236 us; the launch traced here: 232 us
  Pallas kernels  134 us (57%)
  starting transfers between devices  47.8 us (20%)
  waiting for transfers between devices  40.4 us (17%)
  local copies, waits for them, and re-layouts  5.72 us (2%)
  other arithmetic  3.49 us (1%)
    pallas_call x7, Pallas kernels, product_rows(): pl.pallas_call(functools.partial(product_kernel, len(pieces), wide), grid...  115 us
    ppermute x33, starting transfers between devices, send(): return lax.ppermute(data, AXES, route)  47.8 us
    ppermute x33, waiting for transfers between devices, send(): return lax.ppermute(data, AXES, route)  40.4 us
    pallas_call x4, Pallas kernels, column_groups(): pl.pallas_call(functools.partial(columns_kernel, [len(group) for group in...  16.2 us
  transfers between devices with their start and end apart: 33, of which 10 were waited for; matrix products, arithmetic and copies ran while one was open for 2% of the time, Pallas kernels for 51%

profile of v1, /device:TPU:17, one launch (start us, length us, event | category | flops | bytes accessed | tf_op | source)
XLA Modules:
  0.0 231.7 jit_solution(5627193166264779338)
XLA Ops:
  0.0 2.2 copy-done
  2.8 2.4 %smooth_rows.1 = (bf16[256,2048]{1,0:T(8,128)(2,1)S(1)}, bf16[256,2048]{1,0:T(8,128)(2,1)S(1)}, f32[1,2048]{1,0:T(1,128)S(1)}) custom-call(s32[16]{0:T(128)S(1)} %copy-done.3, s32[512,2048]{1,0:T(8,128)S(1)} %copy-done), custom_call_target="tpu_custom_call" | custom-call | flops 1073741824 | bytes 6291456 | tf_op jit(solution)/shard_map/smooth_rows/pallas_call | solution.py:100
  10.4 2.1 collective-permute-start.31
  16.2 1.5 collective-permute-done.4
  17.9 1.6 collective-permute-done.5
  20.7 2.7 %collective-permute-start.23 = (bf16[256,2048]{1,0:T(8,128)(2,1)S(1)}, bf16[256,2048]{1,0:T(8,128)(2,1)}, u32[]{:S(2)}, u32[]{:S(2)}) collective-permute-start(bf16[256,2048]{1,0:T(8,128)(2,1)S(1)} %get-tuple-element.13.refs_0_), channel_id=1, source_target_pairs={{2,4},{3,5},{4,2},{5,3},{10,12},{11,13},{12,10},{13,11},{18,20},{1... | collective-permute-start | bytes 3145736 | tf_op jit(solution)/shard_map/far_0/ppermute | solution.py:301
  23.4 8.0 %collective-permute-done.11.refs_1_ = bf16[256,2048]{1,0:T(8,128)(2,1)} collective-permute-done((bf16[256,2048]{1,0:T(8,128)(2,1)S(1)}, bf16[256,2048]{1,0:T(8,128)(2,1)}, u32[]{:S(2)}, u32[]{:S(2)}) %collective-permute-start.11) | collective-permute-done | bytes 1048608 | tf_op jit(solution)/shard_map/side_0/ppermute | solution.py:301
  31.4 2.3 %collective-permute-start.32 = (bf16[256,2048]{1,0:T(8,128)(2,1)S(1)}, bf16[256,2048]{1,0:T(8,128)(2,1)}, u32[]{:S(2)}, u32[]{:S(2)}) collective-permute-start(bf16[256,2048]{1,0:T(8,128)(2,1)S(1)} %get-tuple-element.14.refs_0_.refs_1_), channel_id=1, source_target_pairs={{0,1},{1,0},{2,3},{3,2},{4,5},{5,4},{6,7},{7,6},{8,9},{9,8},{10,11... | collective-permute-start | bytes 3145736 | tf_op jit(solution)/shard_map/sib_1/ppermute | solution.py:301
  35.0 1.9 collective-permute-start.25
  39.2 3.3 %collective-permute-done.19.refs_0_ = bf16[256,2048]{1,0:T(8,128)(2,1)S(1)} collective-permute-done((bf16[256,2048]{1,0:T(8,128)(2,1)S(1)}, bf16[256,2048]{1,0:T(8,128)(2,1)S(1)}, u32[]{:S(2)}, u32[]{:S(2)}) %collective-permute-start.19) | collective-permute-done | bytes 1048608 | tf_op jit(solution)/shard_map/near_0/ppermute | solution.py:301
  42.7 2.7 %collective-permute-done.23 = bf16[256,2048]{1,0:T(8,128)(2,1)} collective-permute-done((bf16[256,2048]{1,0:T(8,128)(2,1)S(1)}, bf16[256,2048]{1,0:T(8,128)(2,1)}, u32[]{:S(2)}, u32[]{:S(2)}) %collective-permute-start.23) | collective-permute-done | bytes 1048608 | tf_op jit(solution)/shard_map/far_0/ppermute | solution.py:301
  46.1 5.0 %collective-permute-done.12.refs_0_ = bf16[128,2048]{1,0:T(8,128)(2,1)S(1)} collective-permute-done((bf16[128,2048]{1,0:T(8,128)(2,1)S(1)}, bf16[128,2048]{1,0:T(8,128)(2,1)S(1)}, u32[]{:S(2)}, u32[]{:S(2)}) %collective-permute-start.12) | collective-permute-done | bytes 524320 | tf_op jit(solution)/shard_map/corner_0/ppermute | solution.py:301
  51.3 2.5 %collective-permute-done.14.refs_1_ = bf16[128,2048]{1,0:T(8,128)(2,1)S(1)} collective-permute-done((bf16[128,2048]{1,0:T(8,128)(2,1)S(1)}, bf16[128,2048]{1,0:T(8,128)(2,1)S(1)}, u32[]{:S(2)}, u32[]{:S(2)}) %collective-permute-start.14) | collective-permute-done | bytes 524320 | tf_op jit(solution)/shard_map/corner_0/ppermute | solution.py:301
  53.9 1.5 collective-permute-start.24
  56.1 6.5 %column_groups.4.refs_2_ = bf16[2,2,4,128,2048]{4,3,2,1,0:T(8,128)(2,1)S(1)} custom-call(s32[3]{0:T(128)S(1)} %pad_add_fusion.6.place_ref, s32[2]{0:T(128)S(1)} %copy-done.1, f32[1,2048]{1,0:T(1,128)S(1)} %add_multiply_fusion.population_ref, bf16[256,2048]{1,0:T(8,128)(2,1)S(1)} %get-tuple-element.13.refs_0_, ...), custom_call_target="tpu_custom_call" | custom-call | flops 18874368 | bytes 9437184 | tf_op jit(solution)/shard_map/column_groups/pallas_call | solution.py:168
  62.6 2.1 column_groups.5.refs_4_.refs_2_
  65.0 11.8 %collective-permute-start.29 = (bf16[256,2048]{1,0:T(8,128)(2,1)S(1)}, bf16[256,2048]{1,0:T(8,128)(2,1)S(1)}, u32[]{:S(2)}, u32[]{:S(2)}) collective-permute-start(bf16[256,2048]{1,0:T(8,128)(2,1)S(1)} %collective-permute-done.19.refs_0_), channel_id=1, source_target_pairs={{0,1},{1,0},{2,3},{3,2},{4,5},{5,4},{6,7},{7,6},{8,9},{9,8},{10,11... | collective-permute-start | bytes 3145736 | tf_op jit(solution)/shard_map/near_sib_0/ppermute | solution.py:301
  76.9 15.6 %product_rows.7.refs_5_ = bf16[2,4,2,2,256,4,512]{6,5,4,3,2,1,0:T(4,128)(2,1)} custom-call(s32[2]{0:T(128)S(1)} %pad_add_fusion.place_ref, s32[4]{0:T(128)S(1)} %pad_add_fusion.7.spot_ref, f32[1,2048]{1,0:T(1,128)S(1)} %add_multiply_fusion.population_ref, bf16[256,2048]{1,0:T(8,128)(2,1)S(1)} %get-tuple-element.13.refs_0_, ...), custom_call_target="tpu_custom_call" | custom-call | flops 8589934592 | bytes 16777216 | tf_op jit(solution)/shard_map/product_rows/pallas_call | solution.py:251
  92.6 1.9 collective-permute-start.20
  94.5 1.6 collective-permute-start.26
  97.5 3.3 %collective-permute-start.8 = (bf16[256,2048]{1,0:T(8,128)(2,1)}, bf16[256,2048]{1,0:T(8,128)(2,1)S(1)}, u32[]{:S(2)}, u32[]{:S(2)}) collective-permute-start(bf16[256,2048]{1,0:T(8,128)(2,1)} %collective-permute-done.7.refs_1_), channel_id=1, source_target_pairs={{2,4},{3,5},{4,2},{5,3},{10,12},{11,13},{12,10},{13,11},{18,20},{1... | collective-permute-start | bytes 3145736 | tf_op jit(solution)/shard_map/far_near_1/ppermute | solution.py:301
  100.9 5.5 %column_groups.6.refs_2_ = bf16[2,2,4,128,2048]{4,3,2,1,0:T(8,128)(2,1)S(1)} custom-call(s32[3]{0:T(128)S(1)} %pad_add_fusion.6.place_ref, s32[2]{0:T(128)S(1)} %copy-done.1, f32[1,2048]{1,0:T(1,128)S(1)} %add_multiply_fusion.population_ref, bf16[256,2048]{1,0:T(8,128)(2,1)S(1)} %get-tuple-element.14.refs_0_.refs_1_, ...), custom_call_target="tpu_custom_call" | custom-call | flops 18874368 | bytes 9437184 | tf_op jit(solution)/shard_map/column_groups/pallas_call | solution.py:168
  108.0 15.3 %product_rows.8.refs_5_ = bf16[2,4,2,2,256,4,512]{6,5,4,3,2,1,0:T(4,128)(2,1)} custom-call(s32[2]{0:T(128)S(1)} %pad_add_fusion.1.place_ref, s32[4]{0:T(128)S(1)} %pad_add_fusion.7.spot_ref, f32[1,2048]{1,0:T(1,128)S(1)} %add_multiply_fusion.population_ref, bf16[256,2048]{1,0:T(8,128)(2,1)S(1)} %collective-permute-done.19.refs_0_, ...), custom_call_target="tpu_custom_call", output_to_operand_aliasing={{}: (8, {})} | custom-call | flops 8589934592 | bytes 16777216 | tf_op jit(solution)/shard_map/product_rows/pallas_call | solution.py:251
  123.3 1.6 collective-permute-start.27
  127.6 13.6 %collective-permute-done.8 = bf16[256,2048]{1,0:T(8,128)(2,1)S(1)} collective-permute-done((bf16[256,2048]{1,0:T(8,128)(2,1)}, bf16[256,2048]{1,0:T(8,128)(2,1)S(1)}, u32[]{:S(2)}, u32[]{:S(2)}) %collective-permute-start.8) | collective-permute-done | bytes 1048608 | tf_op jit(solution)/shard_map/far_near_1/ppermute | solution.py:301
  142.5 1.8 collective-permute-start.9
  144.3 2.1 column_groups.7.refs_4_.refs_5_.refs_3_
  146.4 15.7 %product_rows.9.refs_5_ = bf16[2,4,2,2,256,4,512]{6,5,4,3,2,1,0:T(4,128)(2,1)} custom-call(s32[2]{0:T(128)S(1)} %pad_add_fusion.place_ref, s32[4]{0:T(128)S(1)} %pad_add_fusion.7.spot_ref, f32[1,2048]{1,0:T(1,128)S(1)} %add_multiply_fusion.population_ref, bf16[256,2048]{1,0:T(8,128)(2,1)S(1)} %get-tuple-element.13.refs_0_, ...), custom_call_target="tpu_custom_call", output_to_operand_aliasing={{}: (8, {})} | custom-call | flops 8589934592 | bytes 16777216 | tf_op jit(solution)/shard_map/product_rows/pallas_call | solution.py:251
  162.1 15.5 %product_rows.10.refs_6_ = bf16[2,4,2,2,256,4,512]{6,5,4,3,2,1,0:T(4,128)(2,1)} custom-call(s32[2]{0:T(128)S(1)} %pad_add_fusion.1.place_ref, s32[4]{0:T(128)S(1)} %pad_add_fusion.7.spot_ref, f32[1,2048]{1,0:T(1,128)S(1)} %add_multiply_fusion.population_ref, bf16[256,2048]{1,0:T(8,128)(2,1)S(1)} %collective-permute-done.19.refs_0_, ...), custom_call_target="tpu_custom_call", output_to_operand_aliasing={{}: (8, {})} | custom-call | flops 8589934592 | bytes 16777216 | tf_op jit(solution)/shard_map/product_rows/pallas_call | solution.py:251
  178.5 24.9 %product_rows.11.refs_4_ = bf16[2,4,2,2,256,4,512]{6,5,4,3,2,1,0:T(4,128)(2,1)} custom-call(s32[2]{0:T(128)S(1)} %pad_add_fusion.2.place_ref, s32[4]{0:T(128)S(1)} %pad_add_fusion.7.spot_ref, f32[1,2048]{1,0:T(1,128)S(1)} %add_multiply_fusion.population_ref, bf16[256,2048]{1,0:T(8,128)(2,1)S(1)} %broadcast_select_fusion.1.refs_0_, ...), custom_call_target="tpu_custom_call", output_to_operand_aliasing={{}: (9, {})} | custom-call | flops 17179869184 | bytes 16777216 | tf_op jit(solution)/shard_map/product_rows/pallas_call | solution.py:251
  203.3 14.2 %product_rows.12.refs_4_ = bf16[2,4,2,2,256,4,512]{6,5,4,3,2,1,0:T(4,128)(2,1)} custom-call(s32[2]{0:T(128)S(1)} %get-tuple-element.15.place_ref, s32[2]{0:T(128)S(1)} %get-tuple-element.16.spot_ref, f32[1,2048]{1,0:T(1,128)S(1)} %add_multiply_fusion.population_ref, ...), custom_call_target="tpu_custom_call", output_to_operand_aliasing={{}: (7, {})} | custom-call | flops 8589934592 | bytes 16777216 | tf_op jit(solution)/shard_map/product_rows/pallas_call | solution.py:251
  217.5 13.9 %product_rows.13 = bf16[2,4,2,2,256,4,512]{6,5,4,3,2,1,0:T(4,128)(2,1)} custom-call(s32[2]{0:T(128)S(1)} %pad_add_fusion.4.place_ref, s32[2]{0:T(128)S(1)} %get-tuple-element.16.spot_ref, f32[1,2048]{1,0:T(1,128)S(1)} %add_multiply_fusion.population_ref, bf16[256,2048]{1,0:T(8,128)(2,1)S(1)} %broadcast_select_fusion.3.refs_0_, ...), custom_call_target="tpu_custom_call", output_to_operand_aliasing={{}: (7, {})} | custom-call | flops 8589934592 | bytes 16777216 | tf_op jit(solution)/shard_map/product_rows/pallas_call | solution.py:251
  (72 shorter events, 24.4 us)
Async XLA Ops:
  5.2 5.2 %collective-permute-start = (f32[1,2048]{1,0:T(1,128)S(1)}, f32[1,2048]{1,0:T(1,128)S(1)}, u32[]{:S(2)}, u32[]{:S(2)}) collective-permute-start(f32[1,2048]{1,0:T(1,128)S(1)} %get-tuple-element.10), channel_id=1, source_target_pairs={{0,8},{1,9},{2,10},{3,11},{4,12},{5,13},{6,14},{7,15},{8,0},{9,1},... | collective-permute-start | bytes 24584 | tf_op jit(solution)/shard_map/sum_rows/ppermute | solution.py:301
  6.5 6.0 %collective-permute-start.1 = (f32[1,2048]{1,0:T(1,128)S(1)}, f32[1,2048]{1,0:T(1,128)S(1)}, u32[]{:S(2)}, u32[]{:S(2)}) collective-permute-start(f32[1,2048]{1,0:T(1,128)S(1)} %get-tuple-element.10), channel_id=1, source_target_pairs={{0,16},{1,17},{2,18},{3,19},{4,20},{5,21},{6,22},{7,23},{8,24},{9,... | collective-permute-start | bytes 24584 | tf_op jit(solution)/shard_map/sum_rows/ppermute | solution.py:301
  7.8 4.7 %collective-permute-start.2 = (f32[1,2048]{1,0:T(1,128)S(1)}, f32[1,2048]{1,0:T(1,128)S(1)}, u32[]{:S(2)}, u32[]{:S(2)}) collective-permute-start(f32[1,2048]{1,0:T(1,128)S(1)} %get-tuple-element.10), channel_id=1, source_target_pairs={{0,24},{1,25},{2,26},{3,27},{4,28},{5,29},{6,30},{7,31},{8,16},{9,... | collective-permute-start | bytes 24584 | tf_op jit(solution)/shard_map/sum_rows/ppermute | solution.py:301
  8.0 23.4 %collective-permute-start.11 = (bf16[256,2048]{1,0:T(8,128)(2,1)S(1)}, bf16[256,2048]{1,0:T(8,128)(2,1)}, u32[]{:S(2)}, u32[]{:S(2)}) collective-permute-start(bf16[256,2048]{1,0:T(8,128)(2,1)S(1)} %get-tuple-element.13.refs_0_), channel_id=1, source_target_pairs={{0,8},{1,9},{2,10},{3,11},{4,12},{5,13},{6,14},{7,15},{8,0},{9,1},... | collective-permute-start | bytes 3145736 | tf_op jit(solution)/shard_map/side_0/ppermute | solution.py:301
  9.2 24.6 %collective-permute-start.13 = (bf16[256,2048]{1,0:T(8,128)(2,1)S(1)}, bf16[256,2048]{1,0:T(8,128)(2,1)}, u32[]{:S(2)}, u32[]{:S(2)}) collective-permute-start(bf16[256,2048]{1,0:T(8,128)(2,1)S(1)} %get-tuple-element.13.refs_0_), channel_id=1, source_target_pairs={{0,16},{1,17},{2,18},{3,19},{4,20},{5,21},{6,22},{7,23},{8,24},{9,... | collective-permute-start | bytes 3145736 | tf_op jit(solution)/shard_map/flank_0/ppermute | solution.py:301
  10.4 24.6 %collective-permute-start.31 = (bf16[256,2048]{1,0:T(8,128)(2,1)S(1)}, bf16[256,2048]{1,0:T(8,128)(2,1)}, u32[]{:S(2)}, u32[]{:S(2)}) collective-permute-start(bf16[256,2048]{1,0:T(8,128)(2,1)S(1)} %get-tuple-element.13.refs_0_), channel_id=1, source_target_pairs={{0,1},{1,0},{2,3},{3,2},{4,5},{5,4},{6,7},{7,6},{8,9},{9,8},{10,11... | collective-permute-start | bytes 3145736 | tf_op jit(solution)/shard_map/sib_0/ppermute | solution.py:301
  14.8 3.0 %collective-permute-start.4 = (f32[1,2048]{1,0:T(1,128)S(1)}, f32[1,2048]{1,0:T(1,128)S(1)}, u32[]{:S(2)}, u32[]{:S(2)}) collective-permute-start(f32[1,2048]{1,0:T(1,128)S(1)} %add.36), channel_id=1, source_target_pairs={{0,2},{1,3},{2,4},{3,5},{4,6},{5,7},{6,0},{7,1},{8,10},{9,11},{10,... | collective-permute-start | bytes 24584 | tf_op jit(solution)/shard_map/sum_line/ppermute | solution.py:301
  16.2 3.4 %collective-permute-start.5 = (f32[1,2048]{1,0:T(1,128)S(1)}, f32[1,2048]{1,0:T(1,128)S(1)}, u32[]{:S(2)}, u32[]{:S(2)}) collective-permute-start(f32[1,2048]{1,0:T(1,128)S(1)} %add.36), channel_id=1, source_target_pairs={{0,4},{1,5},{2,6},{3,7},{4,0},{5,1},{6,2},{7,3},{8,12},{9,13},{10,... | collective-permute-start | bytes 24584 | tf_op jit(solution)/shard_map/sum_line/ppermute | solution.py:301
  17.8 2.9 %collective-permute-start.6 = (f32[1,2048]{1,0:T(1,128)S(1)}, f32[1,2048]{1,0:T(1,128)S(1)}, u32[]{:S(2)}, u32[]{:S(2)}) collective-permute-start(f32[1,2048]{1,0:T(1,128)S(1)} %add.36), channel_id=1, source_target_pairs={{0,6},{1,7},{2,0},{3,1},{4,2},{5,3},{6,4},{7,5},{8,14},{9,15},{10,... | collective-permute-start | bytes 24584 | tf_op jit(solution)/shard_map/sum_line/ppermute | solution.py:301
  19.6 23.0 %collective-permute-start.19 = (bf16[256,2048]{1,0:T(8,128)(2,1)S(1)}, bf16[256,2048]{1,0:T(8,128)(2,1)S(1)}, u32[]{:S(2)}, u32[]{:S(2)}) collective-permute-start(bf16[256,2048]{1,0:T(8,128)(2,1)S(1)} %get-tuple-element.13.refs_0_), channel_id=1, source_target_pairs={{0,2},{1,3},{2,0},{3,1},{4,6},{5,7},{6,4},{7,5},{8,10},{9,11},{10,... | collective-permute-start | bytes 3145736 | tf_op jit(solution)/shard_map/near_0/ppermute | solution.py:301
  20.7 24.8 %collective-permute-start.23 = (bf16[256,2048]{1,0:T(8,128)(2,1)S(1)}, bf16[256,2048]{1,0:T(8,128)(2,1)}, u32[]{:S(2)}, u32[]{:S(2)}) collective-permute-start(bf16[256,2048]{1,0:T(8,128)(2,1)S(1)} %get-tuple-element.13.refs_0_), channel_id=1, source_target_pairs={{2,4},{3,5},{4,2},{5,3},{10,12},{11,13},{12,10},{13,11},{18,20},{1... | collective-permute-start | bytes 3145736 | tf_op jit(solution)/shard_map/far_0/ppermute | solution.py:301
  31.4 33.3 %collective-permute-start.32 = (bf16[256,2048]{1,0:T(8,128)(2,1)S(1)}, bf16[256,2048]{1,0:T(8,128)(2,1)}, u32[]{:S(2)}, u32[]{:S(2)}) collective-permute-start(bf16[256,2048]{1,0:T(8,128)(2,1)S(1)} %get-tuple-element.14.refs_0_.refs_1_), channel_id=1, source_target_pairs={{0,1},{1,0},{2,3},{3,2},{4,5},{5,4},{6,7},{7,6},{8,9},{9,8},{10,11... | collective-permute-start | bytes 3145736 | tf_op jit(solution)/shard_map/sib_1/ppermute | solution.py:301
  33.7 31.3 %collective-permute-start.7 = (bf16[256,2048]{1,0:T(8,128)(2,1)S(1)}, bf16[256,2048]{1,0:T(8,128)(2,1)}, u32[]{:S(2)}, u32[]{:S(2)}) collective-permute-start(bf16[256,2048]{1,0:T(8,128)(2,1)S(1)} %get-tuple-element.14.refs_0_.refs_1_), channel_id=1, source_target_pairs={{0,2},{1,3},{2,0},{3,1},{4,6},{5,7},{6,4},{7,5},{8,10},{9,11},{10,... | collective-permute-start | bytes 3145736 | tf_op jit(solution)/shard_map/near_1/ppermute | solution.py:301
  35.0 41.8 %collective-permute-start.25 = (bf16[256,2048]{1,0:T(8,128)(2,1)S(1)}, bf16[256,2048]{1,0:T(8,128)(2,1)}, u32[]{:S(2)}, u32[]{:S(2)}) collective-permute-start(bf16[256,2048]{1,0:T(8,128)(2,1)S(1)} %get-tuple-element.14.refs_0_.refs_1_), channel_id=1, source_target_pairs={{2,4},{3,5},{4,2},{5,3},{10,12},{11,13},{12,10},{13,11},{18,20},{1... | collective-permute-start | bytes 3145736 | tf_op jit(solution)/shard_map/far_1/ppermute | solution.py:301
  42.5 8.6 %collective-permute-start.12 = (bf16[128,2048]{1,0:T(8,128)(2,1)S(1)}, bf16[128,2048]{1,0:T(8,128)(2,1)S(1)}, u32[]{:S(2)}, u32[]{:S(2)}) collective-permute-start(bf16[128,2048]{1,0:T(8,128)(2,1)S(1)} %slice.19), channel_id=1, source_target_pairs={{0,16},{1,17},{2,18},{3,19},{4,20},{5,21},{6,22},{7,23},{8,24},{9,... | collective-permute-start | bytes 1572872 | tf_op jit(solution)/shard_map/corner_0/ppermute | solution.py:301
  45.4 8.4 %collective-permute-start.14 = (bf16[128,2048]{1,0:T(8,128)(2,1)S(1)}, bf16[128,2048]{1,0:T(8,128)(2,1)S(1)}, u32[]{:S(2)}, u32[]{:S(2)}) collective-permute-start(bf16[128,2048]{1,0:T(8,128)(2,1)S(1)} %slice.20), channel_id=1, source_target_pairs={{0,8},{1,9},{2,10},{3,11},{4,12},{5,13},{6,14},{7,15},{8,0},{9,1},... | collective-permute-start | bytes 1572872 | tf_op jit(solution)/shard_map/corner_0/ppermute | solution.py:301
  51.1 41.5 %collective-permute-start.15 = (bf16[256,2048]{1,0:T(8,128)(2,1)S(1)}, bf16[256,2048]{1,0:T(8,128)(2,1)S(1)}, u32[]{:S(2)}, u32[]{:S(2)}) collective-permute-start(bf16[256,2048]{1,0:T(8,128)(2,1)S(1)} %get-tuple-element.14.refs_0_.refs_1_), channel_id=1, source_target_pairs={{0,8},{1,9},{2,10},{3,11},{4,12},{5,13},{6,14},{7,15},{8,0},{9,1},... | collective-permute-start | bytes 3145736 | tf_op jit(solution)/shard_map/side_1/ppermute | solution.py:301
  53.9 40.7 %collective-permute-start.24 = (bf16[256,2048]{1,0:T(8,128)(2,1)}, bf16[256,2048]{1,0:T(8,128)(2,1)S(1)}, u32[]{:S(2)}, u32[]{:S(2)}) collective-permute-start(bf16[256,2048]{1,0:T(8,128)(2,1)} %collective-permute-done.23), channel_id=1, source_target_pairs={{2,0},{3,1},{4,6},{5,7},{10,8},{11,9},{12,14},{13,15},{18,16},{19,... | collective-permute-start | bytes 3145736 | tf_op jit(solution)/shard_map/out_far_0/ppermute | solution.py:301
  64.7 32.8 %collective-permute-start.17 = (bf16[256,2048]{1,0:T(8,128)(2,1)S(1)}, bf16[256,2048]{1,0:T(8,128)(2,1)S(1)}, u32[]{:S(2)}, u32[]{:S(2)}) collective-permute-start(bf16[256,2048]{1,0:T(8,128)(2,1)S(1)} %get-tuple-element.14.refs_0_.refs_1_), channel_id=1, source_target_pairs={{0,16},{1,17},{2,18},{3,19},{4,20},{5,21},{6,22},{7,23},{8,24},{9,... | collective-permute-start | bytes 3145736 | tf_op jit(solution)/shard_map/flank_1/ppermute | solution.py:301
  65.0 41.4 %collective-permute-start.29 = (bf16[256,2048]{1,0:T(8,128)(2,1)S(1)}, bf16[256,2048]{1,0:T(8,128)(2,1)S(1)}, u32[]{:S(2)}, u32[]{:S(2)}) collective-permute-start(bf16[256,2048]{1,0:T(8,128)(2,1)S(1)} %collective-permute-done.19.refs_0_), channel_id=1, source_target_pairs={{0,1},{1,0},{2,3},{3,2},{4,5},{5,4},{6,7},{7,6},{8,9},{9,8},{10,11... | collective-permute-start | bytes 3145736 | tf_op jit(solution)/shard_map/near_sib_0/ppermute | solution.py:301
  76.9 30.9 %collective-permute-start.30 = (bf16[256,2048]{1,0:T(8,128)(2,1)}, bf16[256,2048]{1,0:T(8,128)(2,1)S(1)}, u32[]{:S(2)}, u32[]{:S(2)}) collective-permute-start(bf16[256,2048]{1,0:T(8,128)(2,1)} %collective-permute-done.7.refs_1_), channel_id=1, source_target_pairs={{0,1},{1,0},{2,3},{3,2},{4,5},{5,4},{6,7},{7,6},{8,9},{9,8},{10,11... | collective-permute-start | bytes 3145736 | tf_op jit(solution)/shard_map/near_sib_1/ppermute | solution.py:301
  92.6 30.7 %collective-permute-start.20 = (bf16[256,2048]{1,0:T(8,128)(2,1)S(1)}, bf16[256,2048]{1,0:T(8,128)(2,1)S(1)}, u32[]{:S(2)}, u32[]{:S(2)}) collective-permute-start(bf16[256,2048]{1,0:T(8,128)(2,1)S(1)} %collective-permute-done.19.refs_0_), channel_id=1, source_target_pairs={{2,4},{3,5},{4,2},{5,3},{10,12},{11,13},{12,10},{13,11},{18,20},{1... | collective-permute-start | bytes 3145736 | tf_op jit(solution)/shard_map/far_near_0/ppermute | solution.py:301
  94.5 30.4 %collective-permute-start.26 = (bf16[256,2048]{1,0:T(8,128)(2,1)}, bf16[256,2048]{1,0:T(8,128)(2,1)S(1)}, u32[]{:S(2)}, u32[]{:S(2)}) collective-permute-start(bf16[256,2048]{1,0:T(8,128)(2,1)} %collective-permute-done.25), channel_id=1, source_target_pairs={{2,0},{3,1},{4,6},{5,7},{10,8},{11,9},{12,14},{13,15},{18,16},{19,... | collective-permute-start | bytes 3145736 | tf_op jit(solution)/shard_map/out_far_1/ppermute | solution.py:301
  97.5 43.7 %collective-permute-start.8 = (bf16[256,2048]{1,0:T(8,128)(2,1)}, bf16[256,2048]{1,0:T(8,128)(2,1)S(1)}, u32[]{:S(2)}, u32[]{:S(2)}) collective-permute-start(bf16[256,2048]{1,0:T(8,128)(2,1)} %collective-permute-done.7.refs_1_), channel_id=1, source_target_pairs={{2,4},{3,5},{4,2},{5,3},{10,12},{11,13},{12,10},{13,11},{18,20},{1... | collective-permute-start | bytes 3145736 | tf_op jit(solution)/shard_map/far_near_1/ppermute | solution.py:301
  106.4 36.1 %collective-permute-start.16 = (bf16[128,2048]{1,0:T(8,128)(2,1)S(1)}, bf16[128,2048]{1,0:T(8,128)(2,1)S(1)}, u32[]{:S(2)}, u32[]{:S(2)}) collective-permute-start(bf16[128,2048]{1,0:T(8,128)(2,1)S(1)} %slice.21), channel_id=1, source_target_pairs={{0,16},{1,17},{2,18},{3,19},{4,20},{5,21},{6,22},{7,23},{8,24},{9,... | collective-permute-start | bytes 1572872 | tf_op jit(solution)/shard_map/corner_1/ppermute | solution.py:301
  107.7 36.5 %collective-permute-start.18 = (bf16[128,2048]{1,0:T(8,128)(2,1)S(1)}, bf16[128,2048]{1,0:T(8,128)(2,1)S(1)}, u32[]{:S(2)}, u32[]{:S(2)}) collective-permute-start(bf16[128,2048]{1,0:T(8,128)(2,1)S(1)} %slice.22), channel_id=1, source_target_pairs={{0,8},{1,9},{2,10},{3,11},{4,12},{5,13},{6,14},{7,15},{8,0},{9,1},... | collective-permute-start | bytes 1572872 | tf_op jit(solution)/shard_map/corner_1/ppermute | solution.py:301
  123.3 55.1 %collective-permute-start.27 = (bf16[256,2048]{1,0:T(8,128)(2,1)S(1)}, bf16[256,2048]{1,0:T(8,128)(2,1)S(1)}, u32[]{:S(2)}, u32[]{:S(2)}) collective-permute-start(bf16[256,2048]{1,0:T(8,128)(2,1)S(1)} %broadcast_select_fusion.1.refs_0_), channel_id=1, source_target_pairs={{0,1},{1,0},{2,3},{3,2},{4,5},{5,4},{6,7},{7,6},{8,9},{9,8},{10,11... | collective-permute-start | bytes 3145736 | tf_op jit(solution)/shard_map/second_sib_0/ppermute | solution.py:301
  124.9 52.7 %collective-permute-start.21 = (bf16[256,2048]{1,0:T(8,128)(2,1)S(1)}, bf16[256,2048]{1,0:T(8,128)(2,1)S(1)}, u32[]{:S(2)}, u32[]{:S(2)}) collective-permute-start(bf16[256,2048]{1,0:T(8,128)(2,1)S(1)} %collective-permute-done.20), channel_id=1, source_target_pairs={{2,0},{3,1},{4,6},{5,7},{10,8},{11,9},{12,14},{13,15},{18,16},{19,... | collective-permute-start | bytes 3145736 | tf_op jit(solution)/shard_map/out_far_near_0/ppermute | solution.py:301
  141.2 37.2 %collective-permute-start.28 = (bf16[256,2048]{1,0:T(8,128)(2,1)S(1)}, bf16[256,2048]{1,0:T(8,128)(2,1)S(1)}, u32[]{:S(2)}, u32[]{:S(2)}) collective-permute-start(bf16[256,2048]{1,0:T(8,128)(2,1)S(1)} %broadcast_select_fusion.refs_1_), channel_id=1, source_target_pairs={{0,1},{1,0},{2,3},{3,2},{4,5},{5,4},{6,7},{7,6},{8,9},{9,8},{10,11... | collective-permute-start | bytes 3145736 | tf_op jit(solution)/shard_map/second_sib_1/ppermute | solution.py:301
  142.5 35.3 %collective-permute-start.9 = (bf16[256,2048]{1,0:T(8,128)(2,1)S(1)}, bf16[256,2048]{1,0:T(8,128)(2,1)S(1)}, u32[]{:S(2)}, u32[]{:S(2)}) collective-permute-start(bf16[256,2048]{1,0:T(8,128)(2,1)S(1)} %collective-permute-done.8), channel_id=1, source_target_pairs={{2,0},{3,1},{4,6},{5,7},{10,8},{11,9},{12,14},{13,15},{18,16},{19,... | collective-permute-start | bytes 3145736 | tf_op jit(solution)/shard_map/out_far_near_1/ppermute | solution.py:301
  177.7 25.6 %collective-permute-start.22 = (bf16[256,2048]{1,0:T(8,128)(2,1)S(1)}, bf16[256,2048]{1,0:T(8,128)(2,1)S(1)}, u32[]{:S(2)}, u32[]{:S(2)}) collective-permute-start(bf16[256,2048]{1,0:T(8,128)(2,1)S(1)} %broadcast_select_fusion.2.refs_0_), channel_id=1, source_target_pairs={{0,1},{1,0},{2,3},{3,2},{4,5},{5,4},{6,7},{7,6},{8,9},{9,8},{10,11... | collective-permute-start | bytes 3145736 | tf_op jit(solution)/shard_map/third_sib_0/ppermute | solution.py:301
  177.9 39.6 %collective-permute-start.10 = (bf16[256,2048]{1,0:T(8,128)(2,1)S(1)}, bf16[256,2048]{1,0:T(8,128)(2,1)S(1)}, u32[]{:S(2)}, u32[]{:S(2)}) collective-permute-start(bf16[256,2048]{1,0:T(8,128)(2,1)S(1)} %broadcast_select_fusion.3.refs_0_), channel_id=1, source_target_pairs={{0,1},{1,0},{2,3},{3,2},{4,5},{5,4},{6,7},{7,6},{8,9},{9,8},{10,11... | collective-permute-start | bytes 3145736 | tf_op jit(solution)/shard_map/third_sib_1/ppermute | solution.py:301
  (5 other events, 43.6 us)
